TPU v7x, 32 devices: a whole 2x2x4 slice. The times are simulated.
32 devices in a mesh: dp: 8 (over z, x), tensor: 4 (over y, core).
Axes of the slice: x: 2, y: 2, z: 4, core: 2. Of those that a mesh axis runs over, the one named last changes fastest.
Arguments:
- residual: bfloat16 [64, 64, 4096], P('dp', None, 'tensor'), may hold values from -128 to 128
- queries: bfloat16 [64, 64, 4096], P('dp', None, 'tensor'), may hold values from -30 to 30
- attn_keys: bfloat16 [64, 64, 512], P('dp', None, 'tensor'), may hold values from -6 to 6
- values: bfloat16 [64, 64, 512], P('dp', None, 'tensor'), may hold values from -6 to 6
- out_weight: bfloat16 [4096, 4096], P('tensor'), may hold values from -0.09375 to 0.09375
- norm_gain: float32 [4096], P('tensor'), may hold values from 0.1 to 1.9
- probe_weight: float32 [4096, 64], P('tensor'), may hold values from -0.09375 to 0.09375
- partner_slot: int32 [64], P('dp'), may hold values from 0 to 7, as said below
- patch_list: int32 [64, 64, 2], P('dp', 'tensor'), may hold values from 0 to 63, as said below
- concept_labels: int32 [64, 64], P('dp'), may hold values from 0 to 63
Outputs:
- attn_out: bfloat16 [64, 64, 4096], P('dp', None, 'tensor')
- logits: float32 [64, 64, 64], P('dp')
- probe_grad: float32 [4096, 64], P('tensor')
Inputs may be any that keep to these rules, and one draw needn't show every extreme that they name: Prompt j of device i of dp, for i below 4, is paired with prompt partner_slot of it on device i + 4, and that prompt's partner_slot is j; on each device the values are a permutation. `patch_list`: each entry is (head, position). A prompt's list equals its partner's, entry for entry. Its entries are distinct, and entries k * 16 to (k + 1) * 16 - 1 name heads of the k-th block of 8 consecutive heads.
All inputs are finite; a program needn't handle non-finite values.
Results may differ from a plain program's by a relative error of at most 0.01.
Values may be sent and summed in bfloat16 or wider, within the bound.
A program may use at most 128 MiB of HBM per device.

v0:
```python
import math

import jax
import jax.numpy as jnp
from jax import lax
from jax.sharding import PartitionSpec as P

DW = 4096
HDIM = 128


norm_epsilon = 1e-05


def passed_along(block, axis, distance):
    devices = range(lax.axis_size(axis))
    route = [((i - distance) % len(devices), i) for i in devices]
    return lax.ppermute(block, axis, route)


def attend(queries, attn_keys, values):
    prompt_count = queries.shape[0]
    seq_length = queries.shape[1]
    local_kv = attn_keys.shape[2] // HDIM
    local_heads = queries.shape[2] // HDIM
    group_size = local_heads // local_kv
    query_blocks = queries.reshape(prompt_count, seq_length, local_kv, group_size, HDIM)
    key_blocks = attn_keys.reshape(prompt_count, seq_length, local_kv, HDIM)
    value_blocks = values.reshape(prompt_count, seq_length, local_kv, HDIM)
    scores = jnp.einsum(
        "pqkgd,pskd->pkgqs", query_blocks, key_blocks, preferred_element_type=jnp.float32
    ) / math.sqrt(HDIM)
    causal = jnp.arange(seq_length)[:, None] >= jnp.arange(seq_length)[None, :]
    scores = jnp.where(causal, scores, -jnp.inf)
    highest = jnp.max(scores, axis=-1, keepdims=True)
    exponent = jnp.exp(scores - highest)
    weights = (exponent / jnp.sum(exponent, axis=-1, keepdims=True)).astype(jnp.bfloat16)
    mixed_rows = jnp.einsum(
        "pkgqs,pskd->pqkgd", weights, value_blocks, preferred_element_type=jnp.float32
    )
    return mixed_rows.astype(jnp.bfloat16).reshape(prompt_count, seq_length, local_heads, HDIM)


def per_device(
    residual,
    queries,
    attn_keys,
    values,
    out_weight,
    norm_gain,
    probe_weight,
    partner_slot,
    patch_list,
    concept_labels,
):
    prompt_count = residual.shape[0]
    seq_length = residual.shape[1]
    feature_count = residual.shape[2]
    token_count = prompt_count * seq_length
    heads_out = attend(queries, attn_keys, values)
    local_heads = heads_out.shape[2]
    head_ids = patch_list[..., 0] % local_heads
    pos_ids = patch_list[..., 1]
    row_ids = jnp.broadcast_to(jnp.arange(prompt_count, dtype=jnp.int32)[:, None], head_ids.shape)
    patch_mask = (
        jnp.zeros((prompt_count, seq_length, local_heads), dtype=bool)
        .at[row_ids, pos_ids, head_ids]
        .set(True)
    )
    half_way = lax.axis_size("dp") // 2
    arrived = passed_along(heads_out, "dp", half_way)
    entry_values = arrived[partner_slot][row_ids, pos_ids, head_ids]
    incoming = jnp.zeros_like(heads_out).at[row_ids, pos_ids, head_ids].set(entry_values)
    patched = jnp.where(patch_mask[..., None], incoming, heads_out)
    partial_value = jnp.dot(
        patched.reshape(token_count, -1), out_weight, preferred_element_type=jnp.float32
    )
    attn_local = lax.psum_scatter(
        partial_value.astype(jnp.bfloat16), "tensor", scatter_dimension=1, tiled=True
    )
    hidden = residual.reshape(token_count, feature_count).astype(jnp.float32) + attn_local.astype(
        jnp.float32
    )
    square_local = jnp.sum(hidden * hidden, axis=1)
    scaled = hidden * norm_gain
    square_sum = lax.psum(square_local, "tensor")
    inverse_rms = lax.rsqrt(square_sum / DW + norm_epsilon)
    normed = scaled * inverse_rms[:, None]
    logit_part = jnp.dot(
        normed, probe_weight, precision=lax.Precision.HIGHEST, preferred_element_type=jnp.float32
    )
    logits = lax.psum(logit_part.astype(jnp.bfloat16), "tensor").astype(jnp.float32)
    classes = jnp.arange(probe_weight.shape[1], dtype=jnp.int32)
    target = (concept_labels.reshape(token_count)[:, None] == classes[None, :]).astype(jnp.float32)
    error = jax.nn.sigmoid(logits) - target
    total_tokens = token_count * lax.axis_size("dp")
    grad_local = lax.dot_general(
        normed,
        error,
        (((0,), (0,)), ((), ())),
        precision=lax.Precision.HIGHEST,
        preferred_element_type=jnp.float32,
    ) / math.sqrt(total_tokens)
    probe_grad = lax.psum(grad_local, "dp")
    return (
        attn_local.reshape(prompt_count, seq_length, feature_count),
        logits.reshape(prompt_count, seq_length, -1),
        probe_grad,
    )


def solution(mesh):
    return jax.shard_map(
        per_device,
        mesh=mesh,
        in_specs=(
            P("dp", None, "tensor"),
            P("dp", None, "tensor"),
            P("dp", None, "tensor"),
            P("dp", None, "tensor"),
            P("tensor", None),
            P("tensor"),
            P("tensor", None),
            P("dp"),
            P("dp", "tensor", None),
            P("dp", None),
        ),
        out_specs=(P("dp", None, "tensor"), P("dp", None, None), P("tensor", None)),
        check_vma=False,
    )
```

profile of v0, /device:TPU:0, one launch (start us, length us, event | category | flops | bytes accessed | tf_op | source)
XLA Modules:
  0.0 255.7 jit_solution(14795839589844669173)
XLA Ops:
  7.2 0.0 reduce-scatter.2.cloned.1.call-start
  7.2 1.2 copy-done
  8.4 2.1 fusion.33
  10.5 0.5 fusion
  11.0 0.6 fusion.3
  11.7 4.1 %collective-permute-start = (bf16[8,64,8,128]{3,1,2,0:T(8,128)(2,1)S(1)}, bf16[8,64,8,128]{3,1,2,0:T(8,128)(2,1)S(1)}, u32[]{:S(2)}, u32[]{:S(2)}) collective-permute-start(bf16[8,64,8,128]{3,1,2,0:T(8,128)(2,1)S(1)} %fusion.3), channel_id=1, source_target_pairs={{16,0},{20,4},{24,8},{28,12},{0,16},{4,20},{8,24},{12,28},{17,1},{... | collective-permute-start | bytes 3145736 | tf_op jit(solution)/shard_map/ppermute | solution.py:18
  15.8 0.5 broadcast.168
  16.3 0.7 fusion.32
  17.0 0.1 reshape.81
  17.1 0.1 reshape.87
  17.2 8.5 %scatter_fusion = pred[8,64,8]{1,2,0:T(8,128)(4,1)S(1)} fusion(pred[8,64,8]{1,2,0:T(8,128)(4,1)S(1)} %broadcast_in_dim.23, s32[128]{0:T(128)S(1)} %reshape.87, pred[128]{0:T(512)(128)(4,1)S(1)} %broadcast.130), kind=kCustom, calls=%fused_computation.2 | custom fusion | bytes 1920 | tf_op jit(solution)/shard_map/scatter | solution.py:68
  25.7 35.7 %collective-permute-done = bf16[8,64,8,128]{3,1,2,0:T(8,128)(2,1)S(1)} collective-permute-done((bf16[8,64,8,128]{3,1,2,0:T(8,128)(2,1)S(1)}, bf16[8,64,8,128]{3,1,2,0:T(8,128)(2,1)S(1)}, u32[]{:S(2)}, u32[]{:S(2)}) %collective-permute-start) | collective-permute-done | bytes 1048608 | tf_op jit(solution)/shard_map/ppermute | solution.py:18
  61.4 0.7 gather_fusion
  62.2 0.7 copy.19
  62.9 1.2 gather_fusion.1
  64.1 0.1 broadcast_in_dim.27
  64.2 8.0 %scatter_fusion.1 = bf16[8,64,8,128]{3,2,1,0:T(8,128)(2,1)S(1)} fusion(bf16[8,64,8,128]{3,2,1,0:T(8,128)(2,1)S(1)} %broadcast_in_dim.27, s32[128]{0:T(128)S(1)} %reshape.87, bf16[128,128]{1,0:T(8,128)(2,1)S(1)} %gather_fusion.1), kind=kCustom, calls=%fused_computation.3 | custom fusion | bytes 99840 | tf_op jit(solution)/shard_map/scatter | solution.py:73
  72.3 1.8 copy_select_fusion
  74.0 0.7 copy.21
  74.7 9.4 %convolution_convert_fusion = bf16[512,4096]{1,0:T(8,128)(2,1)} fusion(bf16[1024,4096]{1,0:T(8,128)(2,1)} %param.14, bf16[64,8,8,128]{3,2,1,0:T(8,128)(2,1)S(1)} %bitcast.52), kind=kOutput, calls=%fused_computation.4 | convolution fusion | flops 4297064448 | bytes 13631488 | tf_op jit(solution)/shard_map/dot_general | solution.py:75
  84.2 0.0 all-reduce.3.cloned.1.call-start
  84.2 45.8 %reduce-scatter.2.cloned.1.call-done = bf16[512,1024]{1,0:T(8,128)(2,1)} async-done(((bf16[512,4096]{1,0:T(8,128)(2,1)}), bf16[512,1024]{1,0:T(8,128)(2,1)}) %reduce-scatter.2.cloned.1.call-update) | async-done | bytes 1048592 | tf_op jit(solution)/shard_map/reduce_scatter | solution.py:78
  130.0 1.7 multiply_reduce_fusion
  131.8 5.8 %psum.21 = f32[512]{0:T(512)S(1)} all-reduce(f32[512]{0:T(512)S(1)} %multiply_reduce_fusion), channel_id=1, replica_groups=mesh['dp'=8,'tensor'=4] {'tensor'}, use_global_device_ids=true, to_apply=%region_6.7 | all-reduce | flops 512 | bytes 4096 | tf_op jit(solution)/shard_map/psum | solution.py:86
  137.5 3.1 %fusion.5 = bf16[512,64]{0,1:T(8,128)(2,1)} fusion(f32[1024,64]{0,1:T(8,128)S(1)} %copy-done.7, bf16[512,1024]{1,0:T(8,128)(2,1)S(1)} %copy-done.3, bf16[512,1024]{1,0:T(8,128)(2,1)S(1)} %bitcast.49, f32[512]{0:T(512)S(1)} %add_rsqrt_fusion, f32[1024]{0:T(1024)S(1)} %copy-done.9), kind=kOutput, calls=%fused_computation.17 | convolution fusion | flops 405307392 | bytes 2430976 | tf_op jit(solution)/shard_map/dot_general | solution.py:89
  140.7 0.0 all-reduce.5.cloned.1.call-start
  140.7 0.1 eq.17
  140.8 32.2 %all-reduce.3.cloned.1.call-done = bf16[512,64]{0,1:T(8,128)(2,1)} async-done(((bf16[512,64]{0,1:T(8,128)(2,1)}), bf16[512,64]{0,1:T(8,128)(2,1)}) %all-reduce.3.cloned.1.call-update) | async-done | bytes 65552 | tf_op jit(solution)/shard_map/psum | solution.py:92
  173.0 3.5 %fusion.4 = f32[1024,64]{0,1:T(8,128)} fusion(bf16[512,1024]{1,0:T(8,128)(2,1)S(1)} %copy-done.3, bf16[512,1024]{1,0:T(8,128)(2,1)S(1)} %bitcast.50, f32[512]{0:T(512)S(1)} %add_rsqrt_fusion, f32[1024]{0:T(1024)S(1)} %copy-done.9, s32[512]{0:T(512)S(1)} %eq.17, bf16[512,64]{0,1:T(8,128)(2,1)} %all-reduce.3.cloned.1.call-done), kind=kOutput, calls=%fused_computation.16 | convolution fusion | flops 405569536 | bytes 2433024 | tf_op jit(solution)/shard_map/dot_general | solution.py:97
  176.5 0.8 copy.26
  177.3 70.2 %all-reduce.5.cloned.1.call-done = f32[1024,64]{0,1:T(8,128)} async-done(((f32[1024,64]{0,1:T(8,128)}), f32[1024,64]{0,1:T(8,128)}) %all-reduce.5.cloned.1.call-update) | async-done | bytes 262160 | tf_op jit(solution)/shard_map/psum | solution.py:104
  247.5 1.7 copy.44
  (31 shorter events, 0.2 us)
Async XLA Ops:
  7.2 1.2 copy-start
  7.2 122.8 %reduce-scatter.2.cloned.1.call-start = ((), (), s32[]{:S(2)}) async-start(), calls=%async_computation.1 | async-start | bytes 5242880 | tf_op jit(solution)/shard_map/reduce_scatter | solution.py:78
  8.4 2.6 %copy-start.8 = (bf16[8,64,128]{2,1,0:T(8,128)(2,1)S(1)}, bf16[8,64,128]{2,1,0:T(8,128)(2,1)}, u32[]{:S(2)}) copy-start(bf16[8,64,128]{2,1,0:T(8,128)(2,1)} %param.13) | copy-start | bytes 393220
  11.0 4.8 %copy-start.5 = (s32[8,16,2]{1,2,0:T(2,128)S(1)}, s32[8,16,2]{1,2,0:T(2,128)}, u32[]{:S(2)}) copy-start(s32[8,16,2]{1,2,0:T(2,128)} %param.18) | copy-start | bytes 3076
  11.7 14.1 %copy-start.1 = (bf16[8,64,8,128]{3,1,2,0:T(8,128)(2,1)}, bf16[8,64,8,128]{3,1,2,0:T(8,128)(2,1)S(1)}, u32[]{:S(2)}) copy-start(bf16[8,64,8,128]{3,1,2,0:T(8,128)(2,1)S(1)} %fusion.3) | copy-start | bytes 3145732
  11.7 14.0 %copy-start.10 = (s32[8]{0:T(128)S(1)}, s32[8]{0:T(128)}, u32[]{:S(2)}) copy-start(s32[8]{0:T(128)} %param.17) | copy-start | bytes 100
  11.7 49.7 %collective-permute-start = (bf16[8,64,8,128]{3,1,2,0:T(8,128)(2,1)S(1)}, bf16[8,64,8,128]{3,1,2,0:T(8,128)(2,1)S(1)}, u32[]{:S(2)}, u32[]{:S(2)}) collective-permute-start(bf16[8,64,8,128]{3,1,2,0:T(8,128)(2,1)S(1)} %fusion.3), channel_id=1, source_target_pairs={{16,0},{20,4},{24,8},{28,12},{0,16},{4,20},{8,24},{12,28},{17,1},{... | collective-permute-start | bytes 3145736 | tf_op jit(solution)/shard_map/ppermute | solution.py:18
  84.1 45.9 %copy-start.2 = (bf16[8,64,1024]{2,1,0:T(8,128)(2,1)S(1)}, bf16[8,64,1024]{2,1,0:T(8,128)(2,1)}, u32[]{:S(2)}) copy-start(bf16[8,64,1024]{2,1,0:T(8,128)(2,1)} %param.10) | copy-start | bytes 3145732
  84.2 53.4 %copy-start.7 = (f32[1024,64]{0,1:T(8,128)S(1)}, f32[1024,64]{0,1:T(8,128)}, u32[]{:S(2)}) copy-start(f32[1024,64]{0,1:T(8,128)} %param.16) | copy-start | bytes 786436
  84.2 53.4 %copy-start.9 = (f32[1024]{0:T(1024)S(1)}, f32[1024]{0:T(1024)}, u32[]{:S(2)}) copy-start(f32[1024]{0:T(1024)} %param.15) | copy-start | bytes 12292
  84.2 56.6 %copy-start.6 = (s32[8,64]{1,0:T(8,128)S(1)}, s32[8,64]{1,0:T(8,128)}, u32[]{:S(2)}) copy-start(s32[8,64]{1,0:T(8,128)} %param.19) | copy-start | bytes 6148
  84.2 88.8 %all-reduce.3.cloned.1.call-start = ((), (), s32[]{:S(2)}) async-start(), calls=%async_computation.2 | async-start | bytes 131072 | tf_op jit(solution)/shard_map/psum | solution.py:92
  130.0 7.5 %copy-start.3 = (bf16[512,1024]{1,0:T(8,128)(2,1)S(1)}, bf16[512,1024]{1,0:T(8,128)(2,1)}, u32[]{:S(2)}) copy-start(bf16[512,1024]{1,0:T(8,128)(2,1)} %reduce-scatter.2.cloned.1.call-done) | copy-start | bytes 3145732
  140.7 106.8 %all-reduce.5.cloned.1.call-start = ((), (), s32[]{:S(2)}) async-start(), calls=%async_computation.3 | async-start | bytes 524288 | tf_op jit(solution)/shard_map/psum | solution.py:104
  173.0 3.5 %copy-start.4 = (bf16[512,64]{0,1:T(8,128)(2,1)S(1)}, bf16[512,64]{0,1:T(8,128)(2,1)}, u32[]{:S(2)}) copy-start(bf16[512,64]{0,1:T(8,128)(2,1)} %all-reduce.3.cloned.1.call-done) | copy-start | bytes 196612
Sparse Core Ops, SparseCore 0:
  84.3 45.6 reduce-scatter.1
  140.8 32.1 all-reduce.2
  176.9 70.5 all-reduce.4
where the time goes:
time: 256 us
  waiting for transfers between devices  184 us (72%)
  local copies, waits for them, and re-layouts  24.5 us (10%)
  matrix products  18.7 us (7%)
  between operations  14 us (5%)
  blocking collectives  5.76 us (2%)
  other arithmetic  4.76 us (2%)
  starting transfers between devices  4.22 us (2%)
    psum x1, waiting for transfers between devices, per_device(): probe_grad = lax.psum(grad_local, 'dp')  70.2 us
    reduce_scatter x1, waiting for transfers between devices, per_device(): lax.psum_scatter(partial_value.astype(jnp.bfloat16), 'tensor', scatter_di...  45.8 us
    ppermute x1, waiting for transfers between devices, passed_along(): return lax.ppermute(block, axis, route)  35.7 us
    psum x1, waiting for transfers between devices, per_device(): lax.psum(logit_part.astype(jnp.bfloat16), 'tensor').astype(jnp.float32)  32.2 us
    dot_general x1, matrix products, per_device(): jnp.dot(patched.reshape(token_count, -1), out_weight, preferred_element_t...  9.4 us
    scatter x1, local copies, waits for them, and re-layouts, per_device(): patch_mask = jnp.zeros((prompt_count, seq_length, local_heads), dtype=boo...  8.48 us
    scatter x1, local copies, waits for them, and re-layouts, per_device(): jnp.zeros_like(heads_out).at[row_ids, pos_ids, head_ids].set(entry_values)  8.03 us
    psum x1, blocking collectives, per_device(): square_sum = lax.psum(square_local, 'tensor')  5.76 us
  transfers between devices with their start and end apart: 4, of which 4 were waited for; matrix products, arithmetic and copies ran while one was open for 4% of the time, Pallas kernels for 0%

commit v1 on v0

v1 whole, which is shorter than its diff:
```python
import functools
import math

import jax
import jax.numpy as jnp
from jax import lax
from jax.experimental import pallas as pl
from jax.experimental.pallas import tpu as pltpu
from jax.sharding import PartitionSpec as P

HDIM = 128
LANES = 128
norm_epsilon = 1e-05
MESH = pl.DeviceIdType.MESH
F32 = jnp.float32
BF16 = jnp.bfloat16


def contract(a, b, dim_a, dim_b):
    return lax.dot_general(
        a, b, (((dim_a,), (dim_b,)), ((), ())), preferred_element_type=F32
    )


def kernel(
    n_dp,
    width,
    slot_ref,
    q_ref,
    k_ref,
    v_ref,
    patch_ref,
    label_ref,
    gain_ref,
    probe_ref,
    weight_hbm,
    residual_hbm,
    out_hbm,
    logits_ref,
    grad_ref,
    w_buf,
    res_buf,
    out_buf,
    heads_buf,
    x_buf,
    entry_send,
    entry_recv,
    a_send,
    a_recv,
    c_send,
    c_recv,
    d_send,
    d_recv,
    own_buf,
    hg_buf,
    probe_buf,
    target_buf,
    err_buf,
    l1_send,
    l1_recv,
    l2_send,
    l2_recv,
    g_send,
    g_recv,
    ag_buf,
    w_sem,
    res_sem,
    out_sem,
    entry_sem,
    a_sems,
    c_sems,
    d_sems,
    l1_sems,
    l2_sems,
    rs_ssem,
    rs_rsem,
    ag_ssem,
    ag_rsem,
):
    prompts, length, features = q_ref.shape
    local_heads = features // HDIM
    classes = probe_ref.shape[1]
    block = res_buf.shape[2]
    d = lax.axis_index("dp")
    t = lax.axis_index("tensor")
    core = lax.rem(t, 2)
    sib = t + 1 - 2 * core
    opp = lax.rem(t + 2, 4)
    opp_sib = lax.rem(sib + 2, 4)
    partner = lax.rem(d + n_dp // 2, n_dp)

    barrier = pltpu.get_barrier_semaphore()
    pl.semaphore_signal(barrier, inc=1, device_id=(d, sib), device_id_type=MESH)
    pl.semaphore_signal(barrier, inc=1, device_id=(d, opp), device_id_type=MESH)
    for off in range(1, n_dp):
        pl.semaphore_signal(
            barrier, inc=1, device_id=(lax.rem(d + off, n_dp), t), device_id_type=MESH
        )

    w_copies = []
    for place, owner in enumerate((opp_sib, opp, sib, t)):
        columns = pl.ds(pl.multiple_of(owner * block, block), block)
        copy = pltpu.make_async_copy(
            weight_hbm.at[:, columns], w_buf.at[place], w_sem.at[place]
        )
        copy.start()
        w_copies.append(copy)
    res_copy = pltpu.make_async_copy(residual_hbm, res_buf, res_sem)
    res_copy.start()

    def one_hot(j):
        pairs = patch_ref[j]
        row = (pairs[:, 0:1] - t * local_heads) * length + pairs[:, 1:2]
        spots = lax.broadcasted_iota(jnp.int32, (pairs.shape[0], local_heads * length), 1)
        return jnp.where(spots == row, 1.0, 0.0).astype(BF16)

    rows = local_heads * length
    s_id = lax.broadcasted_iota(jnp.int32, (length, rows), 0)
    i_id = lax.rem(lax.broadcasted_iota(jnp.int32, (length, rows), 1), length)
    causal = s_id <= i_id
    for j in range(prompts):
        q = jnp.concatenate(
            [q_ref[j, :, h * HDIM : (h + 1) * HDIM] for h in range(local_heads)], axis=0
        )
        scores = contract(k_ref[j], q, 1, 1) * (1.0 / math.sqrt(HDIM))
        scores = jnp.where(causal, scores, -jnp.inf)
        exponent = jnp.exp(scores - jnp.max(scores, axis=0, keepdims=True))
        weights = exponent * (1.0 / jnp.sum(exponent, axis=0, keepdims=True))
        heads = contract(weights.astype(BF16), v_ref[j], 0, 0).astype(BF16)
        heads_buf[j] = heads
        entry_send[j] = contract(one_hot(j), heads, 1, 0).astype(BF16)

    pl.semaphore_wait(barrier, n_dp + 1)
    entry_copy = pltpu.make_async_remote_copy(
        src_ref=entry_send,
        dst_ref=entry_recv,
        send_sem=entry_sem.at[0],
        recv_sem=entry_sem.at[1],
        device_id=(partner, t),
        device_id_type=MESH,
    )
    entry_copy.start()

    probe = probe_ref[...].astype(BF16)
    probe_buf[...] = jnp.concatenate([probe, jnp.zeros_like(probe)], axis=1)
    for j in range(prompts):
        class_id = lax.broadcasted_iota(jnp.int32, (classes, length), 0)
        target = jnp.where(class_id == label_ref[j : j + 1, :], 1.0, 0.0)
        target_buf[j] = target.T
    entry_copy.wait()

    for j in range(prompts):
        arrived = entry_recv[slot_ref[j]]
        both = jnp.concatenate([arrived, jnp.ones_like(arrived)], axis=1)
        placed = contract(one_hot(j), both, 0, 0)
        patched = jnp.where(
            placed[:, HDIM:] > 0.5, placed[:, :HDIM], heads_buf[j].astype(F32)
        ).astype(BF16)
        for h in range(local_heads):
            x_buf[j, :, h * HDIM : (h + 1) * HDIM] = patched[h * length : (h + 1) * length]

    def remote(source, target, sems, j, device):
        return pltpu.make_async_remote_copy(
            src_ref=source.at[j],
            dst_ref=target.at[j],
            send_sem=sems.at[0, j],
            recv_sem=sems.at[1, j],
            device_id=(d, device),
            device_id_type=MESH,
        )

    def project(j, place):
        return jnp.dot(x_buf[j], w_buf[place], preferred_element_type=F32).astype(BF16)

    def start_a(j):
        a_send[j] = project(j, 0)
        remote(a_send, a_recv, a_sems, j, sib).start()

    def start_c(j):
        mine = project(j, 1).astype(F32)
        remote(a_send, a_recv, a_sems, j, sib).wait()
        c_send[j] = (mine + a_recv[j].astype(F32)).astype(BF16)
        remote(c_send, c_recv, c_sems, j, opp).start()

    w_copies[0].wait()
    start_a(0)
    w_copies[1].wait()

    def first(j, carry):
        start_a(j + 1)
        start_c(j)
        return carry

    lax.fori_loop(0, prompts - 1, first, 0)
    start_c(prompts - 1)
    w_copies[2].wait()
    w_copies[3].wait()

    def second(j, carry):
        d_send[j] = project(j, 2)
        remote(d_send, d_recv, d_sems, j, sib).start()
        own_buf[j] = project(j, 3)
        return carry

    lax.fori_loop(0, prompts, second, 0)
    res_copy.wait()

    lane = lax.broadcasted_iota(jnp.int32, (length, LANES), 1)

    def pack(part, squares):
        high = squares.astype(BF16).astype(F32)
        part = jnp.where(lane == classes, high, part)
        part = jnp.where(lane == classes + 1, squares - high, part)
        return part.astype(BF16)

    def unpack(message):
        message = message.astype(F32)
        tail = jnp.where((lane == classes) | (lane == classes + 1), message, 0.0)
        return message, jnp.sum(tail, axis=1, keepdims=True)

    def out_copy(j):
        return pltpu.make_async_copy(out_buf.at[j], out_hbm.at[j], out_sem.at[j])

    def stage3(j):
        remote(d_send, d_recv, d_sems, j, sib).wait()
        remote(c_send, c_recv, c_sems, j, opp).wait()
        total = own_buf[j].astype(F32) + d_recv[j].astype(F32) + c_recv[j].astype(F32)
        attn = total.astype(BF16)
        out_buf[j] = attn
        out_copy(j).start()
        hidden = res_buf[j].astype(F32) + attn.astype(F32)
        squares = jnp.sum(hidden * hidden, axis=1, keepdims=True)
        hg = (hidden * gain_ref[...]).astype(BF16)
        hg_buf[pl.ds(pl.multiple_of(j * length, length), length), :] = hg
        part = jnp.dot(hg, probe_buf[...], preferred_element_type=F32)
        l1_send[j] = pack(part, squares)
        remote(l1_send, l1_recv, l1_sems, j, sib).start()

    def stage4(j):
        remote(l1_send, l1_recv, l1_sems, j, sib).wait()
        part_a, squares_a = unpack(l1_send[j])
        part_b, squares_b = unpack(l1_recv[j])
        l2_send[j] = pack(part_a + part_b, squares_a + squares_b)
        remote(l2_send, l2_recv, l2_sems, j, opp).start()

    def stage5(j):
        remote(l2_send, l2_recv, l2_sems, j, opp).wait()
        part_a, squares_a = unpack(l2_send[j])
        part_b, squares_b = unpack(l2_recv[j])
        inverse = lax.rsqrt((squares_a + squares_b) / width + norm_epsilon)
        logits = (part_a + part_b)[:, :classes] * inverse
        logits_ref[j] = logits
        error = jax.nn.sigmoid(logits) - target_buf[j]
        err_buf[pl.ds(pl.multiple_of(j * length, length), length), :] = (
            error * inverse
        ).astype(BF16)

    stage3(0)
    stage3(1)
    stage4(0)

    def third(j, carry):
        stage3(j)
        stage4(j - 1)
        stage5(j - 2)
        return carry

    lax.fori_loop(2, prompts, third, 0)
    last = prompts - 1
    stage5(last - 1)
    stage4(last)
    early = last * length
    grad = contract(err_buf[:early, :], hg_buf[:early, :], 0, 0)
    stage5(last)
    grad = grad + contract(err_buf[early:, :], hg_buf[early:, :], 0, 0)

    piece_rows = g_send.shape[1]
    per_column = classes // piece_rows
    for i in range(n_dp):
        column, row = i // per_column * LANES, i % per_column * piece_rows
        g_send[i] = grad[row : row + piece_rows, column : column + LANES].astype(g_send.dtype)

    def scatter(peer_to, peer_from):
        return pltpu.make_async_remote_copy(
            src_ref=g_send.at[peer_to],
            dst_ref=g_recv.at[peer_from],
            send_sem=rs_ssem.at[peer_to],
            recv_sem=rs_rsem.at[peer_from],
            device_id=(peer_to, t),
            device_id_type=MESH,
        )

    def gather(peer_to, piece):
        return pltpu.make_async_remote_copy(
            src_ref=ag_buf.at[piece],
            dst_ref=ag_buf.at[piece],
            send_sem=ag_ssem.at[peer_to],
            recv_sem=ag_rsem.at[piece],
            device_id=(peer_to, t),
            device_id_type=MESH,
        )

    peers = [lax.rem(d + off, n_dp) for off in range(1, n_dp)]
    for peer in peers:
        scatter(peer, d).start()
    g_recv[d] = g_send[d]
    for peer in peers:
        scatter(peer, peer).wait_recv()
    total = g_recv[0].astype(F32)
    for i in range(1, n_dp):
        total = total + g_recv[i].astype(F32)
    tokens = prompts * length * n_dp
    ag_buf[d] = (total * (1.0 / math.sqrt(tokens))).astype(ag_buf.dtype)
    for peer in peers:
        gather(peer, d).start()
    for peer in peers:
        gather(peer, peer).wait_recv()
    for column in range(features // LANES):
        piece = jnp.concatenate(
            [ag_buf[column * per_column + i].astype(F32) for i in range(per_column)], axis=0
        )
        grad_ref[column * LANES : (column + 1) * LANES, :] = piece.T
    for peer in peers:
        scatter(peer, peer).wait_send()
        gather(peer, d).wait_send()

    def finish(j, carry):
        out_copy(j).wait()
        return carry

    lax.fori_loop(0, prompts, finish, 0)


def per_device(
    residual,
    queries,
    attn_keys,
    values,
    out_weight,
    norm_gain,
    probe_weight,
    partner_slot,
    patch_list,
    concept_labels,
):
    n_dp = lax.axis_size("dp")
    prompts, length, block = residual.shape
    width = out_weight.shape[1]
    features = queries.shape[2]
    classes = probe_weight.shape[1]
    entries = patch_list.shape[1]
    rows = features // HDIM * length
    tokens = prompts * length
    piece_rows = classes * block // LANES // n_dp
    piece_type = BF16 if piece_rows % 16 == 0 else F32
    vmem = pl.BlockSpec(memory_space=pltpu.VMEM)
    smem = pl.BlockSpec(memory_space=pltpu.SMEM)
    anywhere = pl.BlockSpec(memory_space=pl.ANY)
    dma = pltpu.SemaphoreType.DMA
    part = pltpu.VMEM((prompts, length, block), BF16)
    message = pltpu.VMEM((prompts, length, LANES), BF16)
    pieces = pltpu.VMEM((n_dp, piece_rows, LANES), piece_type)
    scratch = [
        pltpu.VMEM((4, features, block), BF16),
        part,
        part,
        pltpu.VMEM((prompts, rows, HDIM), BF16),
        pltpu.VMEM((prompts, length, features), BF16),
        pltpu.VMEM((prompts, entries, HDIM), BF16),
        pltpu.VMEM((prompts, entries, HDIM), BF16),
        part,
        part,
        part,
        part,
        part,
        part,
        part,
        pltpu.VMEM((tokens, block), BF16),
        pltpu.VMEM((block, 2 * classes), BF16),
        pltpu.VMEM((prompts, length, classes), F32),
        pltpu.VMEM((tokens, classes), BF16),
        message,
        message,
        message,
        message,
        pieces,
        pieces,
        pieces,
        dma((4,)),
        dma,
        dma((prompts,)),
        dma((2,)),
        dma((2, prompts)),
        dma((2, prompts)),
        dma((2, prompts)),
        dma((2, prompts)),
        dma((2, prompts)),
        dma((n_dp,)),
        dma((n_dp,)),
        dma((n_dp,)),
        dma((n_dp,)),
    ]
    return pl.pallas_call(
        functools.partial(kernel, n_dp, width),
        out_shape=(
            jax.ShapeDtypeStruct((prompts, length, block), BF16),
            jax.ShapeDtypeStruct((prompts, length, classes), F32),
            jax.ShapeDtypeStruct((block, classes), F32),
        ),
        in_specs=[smem, vmem, vmem, vmem, vmem, vmem, vmem, vmem, anywhere, anywhere],
        out_specs=(anywhere, vmem, vmem),
        scratch_shapes=scratch,
        compiler_params=pltpu.CompilerParams(
            collective_id=0, has_side_effects=True, vmem_limit_bytes=48 * 1024 * 1024
        ),
    )(
        partner_slot,
        queries,
        attn_keys,
        values,
        patch_list,
        concept_labels,
        norm_gain.reshape(1, block),
        probe_weight,
        out_weight,
        residual,
    )


def solution(mesh):
    return jax.shard_map(
        per_device,
        mesh=mesh,
        in_specs=(
            P("dp", None, "tensor"),
            P("dp", None, "tensor"),
            P("dp", None, "tensor"),
            P("dp", None, "tensor"),
            P("tensor", None),
            P("tensor"),
            P("tensor", None),
            P("dp"),
            P("dp", "tensor", None),
            P("dp", None),
        ),
        out_specs=(P("dp", None, "tensor"), P("dp", None, None), P("tensor", None)),
        check_vma=False,
    )
```

time: 256 us -> 75.7 us (0.30)
  waiting for transfers between devices: 184 us -> 0 us
  Pallas kernels: 0 us -> 63.8 us
  matrix products: 18.7 us -> 0 us
  local copies, waits for them, and re-layouts: 24.5 us -> 10.8 us
  between operations: 14 us -> 0.66 us
  blocking collectives: 5.76 us -> 0 us
  other arithmetic: 4.76 us -> 0 us
  starting transfers between devices: 4.22 us -> 0 us
    psum x2 -> x0, waiting for transfers between devices: 102 us -> none  [the longest x1 70.2 us: per_device(): probe_grad = lax.psum(grad_local, 'dp')]
    pallas_call x0 -> x1, Pallas kernels: none -> 63.8 us  [per_device(): pl.pallas_call(functools.partial(kernel, n_dp, width), out_shape=(jax.Sha...]
    reduce_scatter x1 -> x0, waiting for transfers between devices: 45.8 us -> none  [per_device(): lax.psum_scatter(partial_value.astype(jnp.bfloat16), 'tensor', scatter_di...]
    ppermute x1 -> x0, waiting for transfers between devices: 35.7 us -> none  [passed_along(): return lax.ppermute(block, axis, route)]
    dot_general x5 -> x0, matrix products: 18.7 us -> none  [the longest x1 9.4 us: per_device(): jnp.dot(patched.reshape(token_count, -1), out_weight, preferred_element_t...]
    scatter x2 -> x0, local copies, waits for them, and re-layouts: 16.5 us -> none  [the longest x1 8.48 us: per_device(): patch_mask = jnp.zeros((prompt_count, seq_length, local_heads), dtype=boo...]
    unnamed x24 -> x18, local copies, waits for them, and re-layouts: 3.69 us -> 9.91 us
    psum x1 -> x0, blocking collectives: 5.76 us -> none  [per_device(): square_sum = lax.psum(square_local, 'tensor')]
  transfers between devices with their start and end apart: 4 -> 0, of which waited for: 4 -> 0; matrix products, arithmetic and copies ran while one was open for 4% -> 0% of each run, Pallas kernels for 0% -> 0%
where the time goes in v1:
time: 75.7 us; the launch traced here: 75.3 us
  Pallas kernels  63.8 us (84%)
  local copies, waits for them, and re-layouts  10.8 us (14%)
    pallas_call x1, Pallas kernels, per_device(): pl.pallas_call(functools.partial(kernel, n_dp, width), out_shape=(jax.Sha...  63.8 us
    unnamed x18, local copies, waits for them, and re-layouts  9.91 us

profile of v1, /device:TPU:0, one launch (start us, length us, event | category | flops | bytes accessed | tf_op | source)
XLA Modules:
  0.0 75.3 jit_solution(6226135077711837903)
XLA Ops:
  0.6 0.8 %copy.13.patch_ref = s32[8,16,2]{2,1,0:T(8,128)S(1)} copy(s32[8,16,2]{1,2,0:T(2,128)} %param.18) | data formatting | bytes 2048 | tf_op args[8]
  1.4 1.1 %copy.14.probe_ref = f32[1024,64]{1,0:T(8,128)S(1)} copy(f32[1024,64]{0,1:T(8,128)} %param.16) | data formatting | bytes 524288 | tf_op args[6]
  2.6 0.0 copy-start
  2.6 1.2 %copy-done = bf16[8,64,1024]{2,1,0:T(8,128)(2,1)S(1)} copy-done((bf16[8,64,1024]{2,1,0:T(8,128)(2,1)S(1)}, bf16[8,64,1024]{2,1,0:T(8,128)(2,1)}, u32[]{:S(2)}) %copy-start) | copy-done | bytes 1048600
  3.8 0.0 copy-start.1
  3.8 1.2 %copy-done.1 = bf16[8,64,1024]{2,1,0:T(8,128)(2,1)S(1)} copy-done((bf16[8,64,1024]{2,1,0:T(8,128)(2,1)S(1)}, bf16[8,64,1024]{2,1,0:T(8,128)(2,1)}, u32[]{:S(2)}) %copy-start.1) | copy-done | bytes 1048600
  5.1 0.0 copy-start.2
  5.1 0.9 %copy-done.2 = bf16[8,64,128]{2,1,0:T(8,128)(2,1)S(1)} copy-done((bf16[8,64,128]{2,1,0:T(8,128)(2,1)S(1)}, bf16[8,64,128]{2,1,0:T(8,128)(2,1)}, u32[]{:S(2)}) %copy-start.2) | copy-done | bytes 131096
  6.0 0.0 copy-start.3
  6.0 0.9 %copy-done.3 = bf16[8,64,128]{2,1,0:T(8,128)(2,1)S(1)} copy-done((bf16[8,64,128]{2,1,0:T(8,128)(2,1)S(1)}, bf16[8,64,128]{2,1,0:T(8,128)(2,1)}, u32[]{:S(2)}) %copy-start.3) | copy-done | bytes 131096
  6.9 0.0 copy-start.4
  6.9 0.7 copy-done.4
  7.5 0.0 copy-start.5
  7.5 0.7 copy-done.5
  8.2 0.0 copy-start.6
  8.2 0.7 copy-done.6
  8.9 63.8 %shard_map.121 = (bf16[8,64,1024]{2,1,0:T(8,128)(2,1)S(1)}, f32[8,64,64]{2,1,0:T(8,128)S(1)}, f32[1024,64]{1,0:T(8,128)S(1)}) custom-call(s32[8]{0:T(128)S(1)} %copy-done.6, bf16[8,64,1024]{2,1,0:T(8,128)(2,1)S(1)} %copy-done, bf16[8,64,128]{2,1,0:T(8,128)(2,1)S(1)} %copy-done.2, bf16[8,64,128]{2,1,0:T(8,128)(2,1)S(1)} %copy-done.3, ...), custom_call_target="tpu_custom_call" | custom-call | tf_op jit(solution)/shard_map/pallas_call | solution.py:403
  72.7 0.9 %copy.15 = f32[1024,64]{0,1:T(8,128)} copy(f32[1024,64]{1,0:T(8,128)S(1)} %get-tuple-element.5) | data formatting | bytes 524288 | tf_op jit(solution)/shard_map/pallas_call | solution.py:403
  73.6 1.0 %copy.18 = bf16[8,64,1024]{2,1,0:T(8,128)(2,1)} copy(bf16[8,64,1024]{2,1,0:T(8,128)(2,1)S(1)} %get-tuple-element.9) | data formatting | bytes 2097152
  74.6 0.7 copy.19
Async XLA Ops:
  2.6 1.2 %copy-start = (bf16[8,64,1024]{2,1,0:T(8,128)(2,1)S(1)}, bf16[8,64,1024]{2,1,0:T(8,128)(2,1)}, u32[]{:S(2)}) copy-start(bf16[8,64,1024]{2,1,0:T(8,128)(2,1)} %q_ref.1) | copy-start | bytes 3145732
  3.8 1.2 %copy-start.1 = (bf16[8,64,1024]{2,1,0:T(8,128)(2,1)S(1)}, bf16[8,64,1024]{2,1,0:T(8,128)(2,1)}, u32[]{:S(2)}) copy-start(bf16[8,64,1024]{2,1,0:T(8,128)(2,1)} %residual_hbm.1) | copy-start | bytes 3145732
  5.1 0.9 %copy-start.2 = (bf16[8,64,128]{2,1,0:T(8,128)(2,1)S(1)}, bf16[8,64,128]{2,1,0:T(8,128)(2,1)}, u32[]{:S(2)}) copy-start(bf16[8,64,128]{2,1,0:T(8,128)(2,1)} %k_ref.1) | copy-start | bytes 393220
  6.0 0.9 %copy-start.3 = (bf16[8,64,128]{2,1,0:T(8,128)(2,1)S(1)}, bf16[8,64,128]{2,1,0:T(8,128)(2,1)}, u32[]{:S(2)}) copy-start(bf16[8,64,128]{2,1,0:T(8,128)(2,1)} %v_ref.1) | copy-start | bytes 393220
  6.9 0.7 copy-start.4
  7.5 0.7 copy-start.5
  8.2 0.7 copy-start.6

commit v2 on v1

v2 whole, which is shorter than its diff:
```python
import functools
import math

import jax
import jax.numpy as jnp
from jax import lax
from jax.experimental import pallas as pl
from jax.experimental.pallas import tpu as pltpu
from jax.sharding import PartitionSpec as P

HDIM = 128
LANES = 128
norm_epsilon = 1e-05
MESH = pl.DeviceIdType.MESH
F32 = jnp.float32
BF16 = jnp.bfloat16


def contract(a, b, dim_a, dim_b):
    return lax.dot_general(
        a, b, (((dim_a,), (dim_b,)), ((), ())), preferred_element_type=F32
    )


def kernel(
    n_dp,
    width,
    length,
    slot_hbm,
    q_hbm,
    k_hbm,
    v_hbm,
    patch_hbm,
    label_hbm,
    gain_hbm,
    probe_hbm,
    weight_hbm,
    residual_hbm,
    out_hbm,
    logits_hbm,
    grad_hbm,
    slot_ref,
    q_ref,
    k_ref,
    v_ref,
    patch_ref,
    label_ref,
    gain_ref,
    probe_ref,
    w_buf,
    res_buf,
    out_buf,
    logits_ref,
    grad_ref,
    heads_buf,
    x_buf,
    entry_send,
    entry_recv,
    a_send,
    a_recv,
    c_send,
    c_recv,
    d_send,
    d_recv,
    own_buf,
    hg_buf,
    probe_buf,
    target_buf,
    err_buf,
    l1_send,
    l1_recv,
    l2_send,
    l2_recv,
    g_send,
    g_recv,
    ag_buf,
    in_sem,
    w_sem,
    out_sem,
    logits_sem,
    entry_sem,
    a_sems,
    c_sems,
    d_sems,
    l1_sems,
    l2_sems,
    rs_ssem,
    rs_rsem,
    ag_ssem,
    ag_rsem,
):
    prompts = k_ref.shape[0]
    tokens, features = q_ref.shape
    local_heads = features // HDIM
    classes = probe_ref.shape[0]
    block = res_buf.shape[1]
    d = lax.axis_index("dp")
    t = lax.axis_index("tensor")
    core = lax.rem(t, 2)
    sib = t + 1 - 2 * core
    opp = lax.rem(t + 2, 4)
    opp_sib = lax.rem(sib + 2, 4)
    partner = lax.rem(d + n_dp // 2, n_dp)

    barrier = pltpu.get_barrier_semaphore()
    pl.semaphore_signal(barrier, inc=1, device_id=(d, sib), device_id_type=MESH)
    pl.semaphore_signal(barrier, inc=1, device_id=(d, opp), device_id_type=MESH)
    for off in range(1, n_dp):
        pl.semaphore_signal(
            barrier, inc=1, device_id=(lax.rem(d + off, n_dp), t), device_id_type=MESH
        )

    in_copies = []
    for place, (source, target) in enumerate(
        (
            (patch_hbm, patch_ref),
            (q_hbm, q_ref),
            (k_hbm, k_ref),
            (v_hbm, v_ref),
            (slot_hbm, slot_ref),
            (label_hbm, label_ref),
            (probe_hbm, probe_ref),
            (gain_hbm, gain_ref),
            (residual_hbm, res_buf),
        )
    ):
        copy = pltpu.make_async_copy(source, target, in_sem.at[place])
        in_copies.append(copy)
    w_copies = []
    for place, owner in enumerate((opp_sib, opp, sib, t)):
        columns = pl.ds(pl.multiple_of(owner * block, block), block)
        copy = pltpu.make_async_copy(
            weight_hbm.at[:, columns], w_buf.at[place], w_sem.at[place]
        )
        w_copies.append(copy)
    for copy in in_copies[:8] + w_copies + in_copies[8:]:
        copy.start()

    rows = local_heads * length
    spots = lax.broadcasted_iota(jnp.int32, (rows, patch_ref.shape[2]), 0)

    def one_hot(j):
        pairs = patch_ref[j]
        row = (pairs[0:1, :] - t * local_heads) * length + pairs[1:2, :]
        return jnp.where(spots == row, 1.0, 0.0).astype(BF16)

    def queries_of(j):
        low = j * length
        return jnp.concatenate(
            [
                q_ref[low : low + length, h * HDIM : (h + 1) * HDIM]
                for h in range(local_heads)
            ],
            axis=0,
        )

    def weights_of(scores, causal):
        scores = jnp.where(causal, scores * (1.0 / math.sqrt(HDIM)), -jnp.inf)
        exponent = jnp.exp(scores - jnp.max(scores, axis=0, keepdims=True))
        total = jnp.sum(exponent, axis=0, keepdims=True)
        return (exponent * (1.0 / total)).astype(BF16)

    every = range(prompts)
    for copy in in_copies[:4]:
        copy.wait()
    picked = [contract(one_hot(j), queries_of(j), 0, 0).astype(BF16) for j in every]
    scores = [contract(k_ref[j], picked[j], 1, 1) for j in every]
    s_id = lax.broadcasted_iota(jnp.int32, scores[0].shape, 0)
    weights = [weights_of(scores[j], s_id <= patch_ref[j][1:2, :]) for j in every]
    for j in every:
        entry_send[j] = contract(weights[j], v_ref[j], 0, 0).astype(BF16)

    pl.semaphore_wait(barrier, n_dp + 1)
    entry_copy = pltpu.make_async_remote_copy(
        src_ref=entry_send,
        dst_ref=entry_recv,
        send_sem=entry_sem.at[0],
        recv_sem=entry_sem.at[1],
        device_id=(partner, t),
        device_id_type=MESH,
    )
    entry_copy.start()

    s_id = lax.broadcasted_iota(jnp.int32, (length, rows), 0)
    i_id = lax.rem(lax.broadcasted_iota(jnp.int32, (length, rows), 1), length)
    causal = s_id <= i_id
    for low in range(0, prompts, 2):
        some = range(low, min(low + 2, prompts))
        scores = [contract(k_ref[j], queries_of(j), 1, 1) for j in some]
        weights = [weights_of(part, causal) for part in scores]
        for j, part in zip(some, weights):
            heads_buf[j] = contract(part, v_ref[j], 0, 0).astype(BF16)

    for copy in in_copies[4:8]:
        copy.wait()
    probe = probe_ref[...].astype(BF16)
    probe_buf[...] = jnp.concatenate([probe, jnp.zeros_like(probe)], axis=0)
    for j in every:
        class_id = lax.broadcasted_iota(jnp.int32, (classes, length), 0)
        target = jnp.where(class_id == label_ref[j : j + 1, :], 1.0, 0.0)
        target_buf[j] = target.T
    entry_copy.wait()

    def patch(j):
        arrived = entry_recv[slot_ref[j]]
        both = jnp.concatenate([arrived, jnp.ones_like(arrived)], axis=1)
        placed = contract(one_hot(j), both, 1, 0)
        patched = jnp.where(
            placed[:, HDIM:] > 0.5, placed[:, :HDIM], heads_buf[j].astype(F32)
        ).astype(BF16)
        for h in range(local_heads):
            x_buf[chunk(j), h * HDIM : (h + 1) * HDIM] = patched[
                h * length : (h + 1) * length
            ]

    def chunk(j):
        return pl.ds(pl.multiple_of(j * length, length), length)

    def remote(source, target, sems, j, device, place=None):
        place = chunk(j) if place is None else place
        return pltpu.make_async_remote_copy(
            src_ref=source.at[place],
            dst_ref=target.at[place],
            send_sem=sems.at[0, j],
            recv_sem=sems.at[1, j],
            device_id=(d, device),
            device_id_type=MESH,
        )

    def project(rows, place):
        return jnp.dot(x_buf[rows, :], w_buf[place], preferred_element_type=F32).astype(BF16)

    def start_a(j):
        a_send[chunk(j), :] = project(chunk(j), 0)
        remote(a_send, a_recv, a_sems, j, sib).start()

    def start_c(j):
        mine = project(chunk(j), 1).astype(F32)
        remote(a_send, a_recv, a_sems, j, sib).wait()
        c_send[chunk(j), :] = (mine + a_recv[chunk(j), :].astype(F32)).astype(BF16)
        remote(c_send, c_recv, c_sems, j, opp).start()

    patch(0)
    w_copies[0].wait()
    start_a(0)
    w_copies[1].wait()

    def first(j, carry):
        patch(j + 1)
        start_a(j + 1)
        start_c(j)
        return carry

    lax.fori_loop(0, prompts - 1, first, 0)
    start_c(prompts - 1)
    w_copies[2].wait()
    w_copies[3].wait()
    halves = d_sems.shape[1]
    half = tokens // halves

    def d_copy(j):
        place = pl.ds(pl.multiple_of(j * half, half), half)
        return remote(d_send, d_recv, d_sems, j, sib, place)

    def second(j, carry):
        place = pl.ds(pl.multiple_of(j * half, half), half)
        d_send[place, :] = project(place, 2)
        d_copy(j).start()
        own_buf[place, :] = project(place, 3)
        return carry

    lax.fori_loop(0, halves, second, 0)
    in_copies[8].wait()
    for j in range(halves):
        d_copy(j).wait()

    lane = lax.broadcasted_iota(jnp.int32, (length, LANES), 1)

    def pack(part, squares):
        high = squares.astype(BF16).astype(F32)
        part = jnp.where(lane == classes, high, part)
        part = jnp.where(lane == classes + 1, squares - high, part)
        return part.astype(BF16)

    def unpack(message):
        message = message.astype(F32)
        tail = jnp.where((lane == classes) | (lane == classes + 1), message, 0.0)
        return message, jnp.sum(tail, axis=1, keepdims=True)

    def out_copy(j):
        return pltpu.make_async_copy(
            out_buf.at[chunk(j)], out_hbm.at[chunk(j)], out_sem.at[j]
        )

    def logits_copy(j):
        return pltpu.make_async_copy(logits_ref.at[j], logits_hbm.at[j], logits_sem.at[j])

    def stage3(j):
        remote(c_send, c_recv, c_sems, j, opp).wait()
        at = chunk(j)
        own = own_buf[at, :].astype(F32) + d_recv[at, :].astype(F32)
        attn = (own + c_recv[at, :].astype(F32)).astype(BF16)
        out_buf[at, :] = attn
        out_copy(j).start()
        hidden = res_buf[at, :].astype(F32) + attn.astype(F32)
        squares = jnp.sum(hidden * hidden, axis=1, keepdims=True)
        hg = (hidden * gain_ref[...]).astype(BF16)
        hg_buf[at, :] = hg
        part = contract(hg, probe_buf[...], 1, 1)
        l1_send[j] = pack(part, squares)
        remote(l1_send, l1_recv, l1_sems, j, sib, j).start()

    def stage4(j):
        remote(l1_send, l1_recv, l1_sems, j, sib, j).wait()
        part_a, squares_a = unpack(l1_send[j])
        part_b, squares_b = unpack(l1_recv[j])
        l2_send[j] = pack(part_a + part_b, squares_a + squares_b)
        remote(l2_send, l2_recv, l2_sems, j, opp, j).start()

    def stage5(j):
        remote(l2_send, l2_recv, l2_sems, j, opp, j).wait()
        part_a, squares_a = unpack(l2_send[j])
        part_b, squares_b = unpack(l2_recv[j])
        inverse = lax.rsqrt((squares_a + squares_b) / width + norm_epsilon)
        logits = (part_a + part_b)[:, :classes] * inverse
        logits_ref[j] = logits
        logits_copy(j).start()
        error = jax.nn.sigmoid(logits) - target_buf[j]
        err_buf[chunk(j), :] = (error * inverse).astype(BF16)

    stage3(0)
    stage3(1)
    stage4(0)

    def third(j, carry):
        stage3(j)
        stage4(j - 1)
        stage5(j - 2)
        return carry

    lax.fori_loop(2, prompts, third, 0)
    last = prompts - 1
    stage5(last - 1)
    stage4(last)
    early = last * length
    grad = contract(err_buf[:early, :], hg_buf[:early, :], 0, 0)
    stage5(last)
    grad = grad + contract(err_buf[early:, :], hg_buf[early:, :], 0, 0)

    piece_rows = g_send.shape[1]
    per_column = classes // piece_rows
    for i in range(n_dp):
        column, row = i // per_column * LANES, i % per_column * piece_rows
        g_send[i] = grad[row : row + piece_rows, column : column + LANES].astype(g_send.dtype)

    def scatter(peer_to, peer_from):
        return pltpu.make_async_remote_copy(
            src_ref=g_send.at[peer_to],
            dst_ref=g_recv.at[peer_from],
            send_sem=rs_ssem.at[peer_to],
            recv_sem=rs_rsem.at[peer_from],
            device_id=(peer_to, t),
            device_id_type=MESH,
        )

    def gather(peer_to, piece):
        return pltpu.make_async_remote_copy(
            src_ref=ag_buf.at[piece],
            dst_ref=ag_buf.at[piece],
            send_sem=ag_ssem.at[peer_to],
            recv_sem=ag_rsem.at[piece],
            device_id=(peer_to, t),
            device_id_type=MESH,
        )

    peers = [lax.rem(d + off, n_dp) for off in range(1, n_dp)]
    for peer in peers:
        scatter(peer, d).start()
    g_recv[d] = g_send[d]
    for peer in peers:
        scatter(peer, peer).wait_recv()
    total = g_recv[0].astype(F32)
    for i in range(1, n_dp):
        total = total + g_recv[i].astype(F32)
    ag_buf[d] = (total * (1.0 / math.sqrt(tokens * n_dp))).astype(ag_buf.dtype)
    for peer in peers:
        gather(peer, d).start()
    for peer in peers:
        gather(peer, peer).wait_recv()
    for i in range(n_dp):
        column, row = i // per_column * LANES, i % per_column * piece_rows
        grad_ref[row : row + piece_rows, column : column + LANES] = ag_buf[i].astype(F32)
    grad_copy = pltpu.make_async_copy(grad_ref, grad_hbm, in_sem.at[0])
    grad_copy.start()
    for peer in peers:
        scatter(peer, peer).wait_send()
        gather(peer, d).wait_send()

    def finish(j, carry):
        out_copy(j).wait()
        logits_copy(j).wait()
        return carry

    lax.fori_loop(0, prompts, finish, 0)
    grad_copy.wait()


def per_device(
    residual,
    queries,
    attn_keys,
    values,
    out_weight,
    norm_gain,
    probe_weight,
    partner_slot,
    patch_list,
    concept_labels,
):
    n_dp = lax.axis_size("dp")
    prompts, length, block = residual.shape
    width = out_weight.shape[1]
    features = queries.shape[2]
    classes = probe_weight.shape[1]
    entries = patch_list.shape[1]
    rows = features // HDIM * length
    tokens = prompts * length
    piece_rows = classes * block // LANES // n_dp
    piece_type = BF16 if piece_rows % 16 == 0 else F32
    anywhere = pl.BlockSpec(memory_space=pl.ANY)
    dma = pltpu.SemaphoreType.DMA
    part = pltpu.VMEM((tokens, block), BF16)
    message = pltpu.VMEM((prompts, length, LANES), BF16)
    pieces = pltpu.VMEM((n_dp, piece_rows, LANES), piece_type)
    scratch = [
        pltpu.SMEM((prompts,), jnp.int32),
        pltpu.VMEM((tokens, features), BF16),
        pltpu.VMEM(attn_keys.shape, BF16),
        pltpu.VMEM(values.shape, BF16),
        pltpu.VMEM((prompts, 2, entries), jnp.int32),
        pltpu.VMEM(concept_labels.shape, jnp.int32),
        pltpu.VMEM((1, block), F32),
        pltpu.VMEM((classes, block), F32),
        pltpu.VMEM((4, features, block), BF16),
        part,
        part,
        pltpu.VMEM((prompts, length, classes), F32),
        pltpu.VMEM((classes, block), F32),
        pltpu.VMEM((prompts, rows, HDIM), BF16),
        pltpu.VMEM((tokens, features), BF16),
        pltpu.VMEM((prompts, entries, HDIM), BF16),
        pltpu.VMEM((prompts, entries, HDIM), BF16),
        part,
        part,
        part,
        part,
        part,
        part,
        part,
        part,
        pltpu.VMEM((2 * classes, block), BF16),
        pltpu.VMEM((prompts, length, classes), F32),
        pltpu.VMEM((tokens, classes), BF16),
        message,
        message,
        message,
        message,
        pieces,
        pieces,
        pieces,
        dma((9,)),
        dma((4,)),
        dma((prompts,)),
        dma((prompts,)),
        dma((2,)),
        dma((2, prompts)),
        dma((2, prompts)),
        dma((2, 2)),
        dma((2, prompts)),
        dma((2, prompts)),
        dma((n_dp,)),
        dma((n_dp,)),
        dma((n_dp,)),
        dma((n_dp,)),
    ]
    attn_out, logits, grad = pl.pallas_call(
        functools.partial(kernel, n_dp, width, length),
        out_shape=(
            jax.ShapeDtypeStruct((tokens, block), BF16),
            jax.ShapeDtypeStruct((prompts, length, classes), F32),
            jax.ShapeDtypeStruct((classes, block), F32),
        ),
        in_specs=[anywhere] * 10,
        out_specs=(anywhere,) * 3,
        scratch_shapes=scratch,
        compiler_params=pltpu.CompilerParams(
            collective_id=0, has_side_effects=True, vmem_limit_bytes=60 * 1024 * 1024
        ),
    )(
        partner_slot,
        queries.reshape(tokens, features),
        attn_keys,
        values,
        jnp.swapaxes(patch_list, 1, 2),
        concept_labels,
        norm_gain.reshape(1, block),
        probe_weight.T,
        out_weight,
        residual.reshape(tokens, block),
    )
    return attn_out.reshape(prompts, length, block), logits, grad.T


def solution(mesh):
    return jax.shard_map(
        per_device,
        mesh=mesh,
        in_specs=(
            P("dp", None, "tensor"),
            P("dp", None, "tensor"),
            P("dp", None, "tensor"),
            P("dp", None, "tensor"),
            P("tensor", None),
            P("tensor"),
            P("tensor", None),
            P("dp"),
            P("dp", "tensor", None),
            P("dp", None),
        ),
        out_specs=(P("dp", None, "tensor"), P("dp", None, None), P("tensor", None)),
        check_vma=False,
    )
```

time: 75.7 us -> 67.9 us (0.90)
  local copies, waits for them, and re-layouts: 10.8 us -> 5.6 us
  Pallas kernels: 63.8 us -> 61.4 us
    unnamed x18 -> x3, local copies, waits for them, and re-layouts: 9.91 us -> 5.6 us
    pallas_call x1, Pallas kernels: 63.8 us -> 61.4 us  [per_device(): pl.pallas_call(functools.partial(kernel, n_dp, width, length), out_shape=...]
    pallas_call x1 -> x0, local copies, waits for them, and re-layouts: 0.89 us -> none  [per_device(): pl.pallas_call(functools.partial(kernel, n_dp, width), out_shape=(jax.Sha...]
where the time goes in v2:
time: 67.9 us; the launch traced here: 67.7 us
  Pallas kernels  61.4 us (90%)
  local copies, waits for them, and re-layouts  5.6 us (8%)
    pallas_call x1, Pallas kernels, per_device(): pl.pallas_call(functools.partial(kernel, n_dp, width, length), out_shape=...  61.4 us
    unnamed x3, local copies, waits for them, and re-layouts  5.6 us

profile of v2, /device:TPU:0, one launch (start us, length us, event | category | flops | bytes accessed | tf_op | source)
XLA Modules:
  0.0 67.7 jit_solution(8058610585684288951)
XLA Ops:
  0.6 61.4 %shard_map.121 = (bf16[512,1024]{1,0:T(8,128)(2,1)}, f32[8,64,64]{2,1,0:T(8,128)}, f32[64,1024]{1,0:T(8,128)}) custom-call(s32[8]{0:T(128)} %slot_hbm.1, bf16[512,1024]{1,0:T(8,128)(2,1)} %bitcast.8, bf16[8,64,128]{2,1,0:T(8,128)(2,1)} %k_hbm.1, bf16[8,64,128]{2,1,0:T(8,128)(2,1)} %v_hbm.1, s32[8,2,16]{2,1,0:T(2,128)} %bitcast.12, s32[8,64]{1,0:T(8,128)} %label_hbm.1, ...), custom_call_target="tpu_custom_call" | custom-call | tf_op jit(solution)/shard_map/pallas_call | solution.py:486
  62.1 2.3 %copy.16 = bf16[8,64,1024]{2,1,0:T(8,128)(2,1)} copy(bf16[8,64,1024]{2,1,0:T(8,128)(2,1)} %bitcast.7) | data formatting | bytes 2097152
  64.3 1.7 %copy.17 = f32[8,64,64]{2,1,0:T(8,128)} copy(f32[8,64,64]{2,1,0:T(8,128)} %get-tuple-element.13) | data formatting | bytes 262144
  66.0 1.7 %copy.18 = f32[1024,64]{0,1:T(8,128)} copy(f32[1024,64]{0,1:T(8,128)} %bitcast.11) | data formatting | bytes 524288

commit v3 on v2

--- a/solution.py
+++ b/solution.py
@@ -10,6 +10,7 @@
 
 HDIM = 128
 LANES = 128
+VMEM_BYTES = 62 * 1024 * 1024
 norm_epsilon = 1e-05
 MESH = pl.DeviceIdType.MESH
 F32 = jnp.float32
@@ -77,7 +78,6 @@
     in_sem,
     w_sem,
     out_sem,
-    logits_sem,
     entry_sem,
     a_sems,
     c_sems,
@@ -287,21 +287,12 @@
         tail = jnp.where((lane == classes) | (lane == classes + 1), message, 0.0)
         return message, jnp.sum(tail, axis=1, keepdims=True)
 
-    def out_copy(j):
-        return pltpu.make_async_copy(
-            out_buf.at[chunk(j)], out_hbm.at[chunk(j)], out_sem.at[j]
-        )
-
-    def logits_copy(j):
-        return pltpu.make_async_copy(logits_ref.at[j], logits_hbm.at[j], logits_sem.at[j])
-
     def stage3(j):
         remote(c_send, c_recv, c_sems, j, opp).wait()
         at = chunk(j)
         own = own_buf[at, :].astype(F32) + d_recv[at, :].astype(F32)
         attn = (own + c_recv[at, :].astype(F32)).astype(BF16)
         out_buf[at, :] = attn
-        out_copy(j).start()
         hidden = res_buf[at, :].astype(F32) + attn.astype(F32)
         squares = jnp.sum(hidden * hidden, axis=1, keepdims=True)
         hg = (hidden * gain_ref[...]).astype(BF16)
@@ -324,27 +315,35 @@
         inverse = lax.rsqrt((squares_a + squares_b) / width + norm_epsilon)
         logits = (part_a + part_b)[:, :classes] * inverse
         logits_ref[j] = logits
-        logits_copy(j).start()
         error = jax.nn.sigmoid(logits) - target_buf[j]
         err_buf[chunk(j), :] = (error * inverse).astype(BF16)
 
+    out_copies = [
+        pltpu.make_async_copy(source, target, out_sem.at[place])
+        for place, (source, target) in enumerate(
+            ((out_buf, out_hbm), (logits_ref, logits_hbm), (grad_ref, grad_hbm))
+        )
+    ]
     stage3(0)
-    stage3(1)
-    stage4(0)
 
     def third(j, carry):
         stage3(j)
         stage4(j - 1)
-        stage5(j - 2)
         return carry
 
-    lax.fori_loop(2, prompts, third, 0)
+    def fourth(j, carry):
+        stage5(j)
+        return carry
+
+    lax.fori_loop(1, prompts, third, 0)
+    out_copies[0].start()
     last = prompts - 1
-    stage5(last - 1)
     stage4(last)
+    lax.fori_loop(0, last, fourth, 0)
     early = last * length
     grad = contract(err_buf[:early, :], hg_buf[:early, :], 0, 0)
     stage5(last)
+    out_copies[1].start()
     grad = grad + contract(err_buf[early:, :], hg_buf[early:, :], 0, 0)
 
     piece_rows = g_send.shape[1]
@@ -390,19 +389,24 @@
     for i in range(n_dp):
         column, row = i // per_column * LANES, i % per_column * piece_rows
         grad_ref[row : row + piece_rows, column : column + LANES] = ag_buf[i].astype(F32)
-    grad_copy = pltpu.make_async_copy(grad_ref, grad_hbm, in_sem.at[0])
-    grad_copy.start()
+    out_copies[2].start()
     for peer in peers:
         scatter(peer, peer).wait_send()
         gather(peer, d).wait_send()
-
-    def finish(j, carry):
-        out_copy(j).wait()
-        logits_copy(j).wait()
-        return carry
-
-    lax.fori_loop(0, prompts, finish, 0)
-    grad_copy.wait()
+    for copy in out_copies:
+        copy.wait()
+
+
+def store_kernel(*refs):
+    count = len(refs) // 2
+    sems = refs[-1]
+    copies = [
+        pltpu.make_async_copy(refs[i], refs[count + i], sems.at[i]) for i in range(count)
+    ]
+    for copy in copies:
+        copy.start()
+    for copy in copies:
+        copy.wait()
 
 
 def per_device(
@@ -470,8 +474,7 @@
         pieces,
         dma((9,)),
         dma((4,)),
-        dma((prompts,)),
-        dma((prompts,)),
+        dma((3,)),
         dma((2,)),
         dma((2, prompts)),
         dma((2, prompts)),
@@ -483,18 +486,19 @@
         dma((n_dp,)),
         dma((n_dp,)),
     ]
-    attn_out, logits, grad = pl.pallas_call(
+    results = (
+        jax.ShapeDtypeStruct((tokens, block), BF16),
+        jax.ShapeDtypeStruct((prompts, length, classes), F32),
+        jax.ShapeDtypeStruct((classes, block), F32),
+    )
+    held = pl.pallas_call(
         functools.partial(kernel, n_dp, width, length),
-        out_shape=(
-            jax.ShapeDtypeStruct((tokens, block), BF16),
-            jax.ShapeDtypeStruct((prompts, length, classes), F32),
-            jax.ShapeDtypeStruct((classes, block), F32),
-        ),
+        out_shape=results,
         in_specs=[anywhere] * 10,
         out_specs=(anywhere,) * 3,
         scratch_shapes=scratch,
         compiler_params=pltpu.CompilerParams(
-            collective_id=0, has_side_effects=True, vmem_limit_bytes=60 * 1024 * 1024
+            collective_id=0, has_side_effects=True, vmem_limit_bytes=VMEM_BYTES
         ),
     )(
         partner_slot,
@@ -508,6 +512,14 @@
         out_weight,
         residual.reshape(tokens, block),
     )
+    attn_out, logits, grad = pl.pallas_call(
+        store_kernel,
+        out_shape=results,
+        in_specs=[anywhere] * 3,
+        out_specs=(anywhere,) * 3,
+        scratch_shapes=[dma((3,))],
+        compiler_params=pltpu.CompilerParams(vmem_limit_bytes=VMEM_BYTES),
+    )(*held)
     return attn_out.reshape(prompts, length, block), logits, grad.T
 
 

time: 67.9 us -> 100 us (1.47)
  Pallas kernels: 61.4 us -> 99.6 us
  local copies, waits for them, and re-layouts: 5.6 us -> 0 us
    pallas_call x0 -> x1, Pallas kernels: none -> 48.8 us  [per_device(): pl.pallas_call(store_kernel, out_shape=results, in_specs=[anywhere] * 3,...]
    pallas_call x1, Pallas kernels: 61.4 us -> 50.9 us  [per_device(): pl.pallas_call(functools.partial(kernel, n_dp, width, length), out_shape=...]
    unnamed x3 -> x0, local copies, waits for them, and re-layouts: 5.6 us -> none
where the time goes in v3:
time: 100 us
  Pallas kernels  99.6 us (100%)
    pallas_call x1, Pallas kernels, per_device(): pl.pallas_call(functools.partial(kernel, n_dp, width, length), out_shape=...  50.9 us
    pallas_call x1, Pallas kernels, per_device(): pl.pallas_call(store_kernel, out_shape=results, in_specs=[anywhere] * 3,...  48.8 us

profile of v3, /device:TPU:0, one launch (start us, length us, event | category | flops | bytes accessed | tf_op | source)
XLA Modules:
  0.0 100.3 jit_solution(14374493229503850504)
XLA Ops:
  0.6 50.9 %shard_map.121 = (bf16[512,1024]{1,0:T(8,128)(2,1)}, f32[8,64,64]{2,1,0:T(8,128)}, f32[64,1024]{1,0:T(8,128)}) custom-call(s32[8]{0:T(128)} %slot_hbm.1, bf16[512,1024]{1,0:T(8,128)(2,1)} %bitcast.7, bf16[8,64,128]{2,1,0:T(8,128)(2,1)} %k_hbm.1, bf16[8,64,128]{2,1,0:T(8,128)(2,1)} %v_hbm.1, s32[8,2,16]{2,1,0:T(2,128)} %bitcast.10, s32[8,64]{1,0:T(8,128)} %label_hbm.1, ...), custom_call_target="tpu_custom_call" | custom-call | tf_op jit(solution)/shard_map/pallas_call | solution.py:494
  51.5 48.8 %shard_map.122 = (bf16[512,1024]{1,0:T(8,128)(2,1)}, f32[8,64,64]{2,1,0:T(8,128)}, f32[64,1024]{1,0:T(8,128)}) custom-call(bf16[512,1024]{1,0:T(8,128)(2,1)} %get-tuple-element.9.refs_0_, f32[8,64,64]{2,1,0:T(8,128)} %get-tuple-element.10.refs_1_, f32[64,1024]{1,0:T(8,128)} %get-tuple-element.11.refs_2_), custom_call_target="tpu_custom_call" | custom-call | tf_op jit(solution)/shard_map/pallas_call | solution.py:515

commit v4 on v3

--- a/solution.py
+++ b/solution.py
@@ -10,6 +10,7 @@
 
 HDIM = 128
 LANES = 128
+STORE_PARTS = 2
 VMEM_BYTES = 62 * 1024 * 1024
 norm_epsilon = 1e-05
 MESH = pl.DeviceIdType.MESH
@@ -161,9 +162,23 @@
         return (exponent * (1.0 / total)).astype(BF16)
 
     every = range(prompts)
+    entries = patch_ref.shape[2]
+    picks = lax.broadcasted_iota(jnp.int32, (entries, rows), 1)
+
+    def one_hot_rows(j):
+        return jnp.where(picks == columns_of[:, j : j + 1], 1.0, 0.0).astype(BF16)
+
     for copy in in_copies[:4]:
         copy.wait()
-    picked = [contract(one_hot(j), queries_of(j), 0, 0).astype(BF16) for j in every]
+    index_rows = jnp.concatenate(
+        [(patch_ref[j][0:1, :] - t * local_heads) * length + patch_ref[j][1:2, :] for j in every],
+        axis=0,
+    )
+    wide = jnp.concatenate(
+        [index_rows, jnp.zeros((prompts, LANES - entries), jnp.int32)], axis=1
+    )
+    columns_of = wide.T[:entries, :]
+    picked = [contract(one_hot_rows(j), queries_of(j), 1, 0).astype(BF16) for j in every]
     scores = [contract(k_ref[j], picked[j], 1, 1) for j in every]
     s_id = lax.broadcasted_iota(jnp.int32, scores[0].shape, 0)
     weights = [weights_of(scores[j], s_id <= patch_ref[j][1:2, :]) for j in every]
@@ -184,21 +199,18 @@
     s_id = lax.broadcasted_iota(jnp.int32, (length, rows), 0)
     i_id = lax.rem(lax.broadcasted_iota(jnp.int32, (length, rows), 1), length)
     causal = s_id <= i_id
-    for low in range(0, prompts, 2):
-        some = range(low, min(low + 2, prompts))
+
+    def attend(low, high):
+        some = range(low, high)
         scores = [contract(k_ref[j], queries_of(j), 1, 1) for j in some]
         weights = [weights_of(part, causal) for part in scores]
         for j, part in zip(some, weights):
             heads_buf[j] = contract(part, v_ref[j], 0, 0).astype(BF16)
 
-    for copy in in_copies[4:8]:
-        copy.wait()
-    probe = probe_ref[...].astype(BF16)
-    probe_buf[...] = jnp.concatenate([probe, jnp.zeros_like(probe)], axis=0)
-    for j in every:
-        class_id = lax.broadcasted_iota(jnp.int32, (classes, length), 0)
-        target = jnp.where(class_id == label_ref[j : j + 1, :], 1.0, 0.0)
-        target_buf[j] = target.T
+    ready = min(4, prompts)
+    for low in range(0, ready, 2):
+        attend(low, min(low + 2, ready))
+    in_copies[4].wait()
     entry_copy.wait()
 
     def patch(j):
@@ -251,7 +263,12 @@
         start_c(j)
         return carry
 
-    lax.fori_loop(0, prompts - 1, first, 0)
+    done = 0
+    for low in range(ready, prompts, 2):
+        first(done, 0)
+        done += 1
+        attend(low, min(low + 2, prompts))
+    lax.fori_loop(done, prompts - 1, first, 0)
     start_c(prompts - 1)
     w_copies[2].wait()
     w_copies[3].wait()
@@ -270,13 +287,19 @@
         return carry
 
     lax.fori_loop(0, halves, second, 0)
-    in_copies[8].wait()
+    for copy in in_copies[5:]:
+        copy.wait()
+    probe = probe_ref[...].astype(BF16)
+    probe_buf[...] = jnp.concatenate([probe, jnp.zeros_like(probe)], axis=0)
+    for j in every:
+        class_id = lax.broadcasted_iota(jnp.int32, (classes, length), 0)
+        target = jnp.where(class_id == label_ref[j : j + 1, :], 1.0, 0.0)
+        target_buf[j] = target.T
     for j in range(halves):
         d_copy(j).wait()
 
-    lane = lax.broadcasted_iota(jnp.int32, (length, LANES), 1)
-
     def pack(part, squares):
+        lane = lax.broadcasted_iota(jnp.int32, part.shape, 1)
         high = squares.astype(BF16).astype(F32)
         part = jnp.where(lane == classes, high, part)
         part = jnp.where(lane == classes + 1, squares - high, part)
@@ -284,6 +307,7 @@
 
     def unpack(message):
         message = message.astype(F32)
+        lane = lax.broadcasted_iota(jnp.int32, message.shape, 1)
         tail = jnp.where((lane == classes) | (lane == classes + 1), message, 0.0)
         return message, jnp.sum(tail, axis=1, keepdims=True)
 
@@ -308,15 +332,17 @@
         l2_send[j] = pack(part_a + part_b, squares_a + squares_b)
         remote(l2_send, l2_recv, l2_sems, j, opp, j).start()
 
-    def stage5(j):
-        remote(l2_send, l2_recv, l2_sems, j, opp, j).wait()
-        part_a, squares_a = unpack(l2_send[j])
-        part_b, squares_b = unpack(l2_recv[j])
+    def stage5(low, high):
+        for j in range(low, high):
+            remote(l2_send, l2_recv, l2_sems, j, opp, j).wait()
+        count = (high - low) * length
+        part_a, squares_a = unpack(l2_send[low:high].reshape(count, LANES))
+        part_b, squares_b = unpack(l2_recv[low:high].reshape(count, LANES))
         inverse = lax.rsqrt((squares_a + squares_b) / width + norm_epsilon)
         logits = (part_a + part_b)[:, :classes] * inverse
-        logits_ref[j] = logits
-        error = jax.nn.sigmoid(logits) - target_buf[j]
-        err_buf[chunk(j), :] = (error * inverse).astype(BF16)
+        logits_ref[low:high] = logits.reshape(high - low, length, classes)
+        error = jax.nn.sigmoid(logits) - target_buf[low:high].reshape(count, classes)
+        err_buf[low * length : high * length, :] = (error * inverse).astype(BF16)
 
     out_copies = [
         pltpu.make_async_copy(source, target, out_sem.at[place])
@@ -331,18 +357,14 @@
         stage4(j - 1)
         return carry
 
-    def fourth(j, carry):
-        stage5(j)
-        return carry
-
     lax.fori_loop(1, prompts, third, 0)
     out_copies[0].start()
     last = prompts - 1
     stage4(last)
-    lax.fori_loop(0, last, fourth, 0)
+    stage5(0, last)
     early = last * length
     grad = contract(err_buf[:early, :], hg_buf[:early, :], 0, 0)
-    stage5(last)
+    stage5(last, prompts)
     out_copies[1].start()
     grad = grad + contract(err_buf[early:, :], hg_buf[early:, :], 0, 0)
 
@@ -397,16 +419,29 @@
         copy.wait()
 
 
-def store_kernel(*refs):
-    count = len(refs) // 2
-    sems = refs[-1]
-    copies = [
-        pltpu.make_async_copy(refs[i], refs[count + i], sems.at[i]) for i in range(count)
-    ]
-    for copy in copies:
-        copy.start()
-    for copy in copies:
-        copy.wait()
+def store_kernel(count, *refs):
+    sources, targets, held = refs[:count], refs[count : 2 * count], refs[2 * count : -2]
+    load_sems, store_sems = refs[-2:]
+    parts = []
+    for source, target, buffer in zip(sources, targets, held):
+        step = source.shape[0] // STORE_PARTS
+        for i in range(STORE_PARTS):
+            at = pl.ds(i * step, step)
+            place = len(parts)
+            load = pltpu.make_async_copy(
+                source.at[at], buffer.at[at], load_sems.at[place]
+            )
+            store = pltpu.make_async_copy(
+                buffer.at[at], target.at[at], store_sems.at[place]
+            )
+            parts.append((load, store))
+    for load, _ in parts:
+        load.start()
+    for load, store in parts:
+        load.wait()
+        store.start()
+    for _, store in parts:
+        store.wait()
 
 
 def per_device(
@@ -513,11 +548,12 @@
         residual.reshape(tokens, block),
     )
     attn_out, logits, grad = pl.pallas_call(
-        store_kernel,
+        functools.partial(store_kernel, len(results)),
         out_shape=results,
         in_specs=[anywhere] * 3,
         out_specs=(anywhere,) * 3,
-        scratch_shapes=[dma((3,))],
+        scratch_shapes=[pltpu.VMEM(result.shape, result.dtype) for result in results]
+        + [dma((len(results) * STORE_PARTS,))] * 2,
         compiler_params=pltpu.CompilerParams(vmem_limit_bytes=VMEM_BYTES),
     )(*held)
     return attn_out.reshape(prompts, length, block), logits, grad.T

time: 100 us -> 53.9 us (0.54)
  Pallas kernels: 99.6 us -> 53.1 us
    pallas_call x1, Pallas kernels: 48.8 us -> 2.28 us  [per_device(): pl.pallas_call(functools.partial(store_kernel, len(results)), out_shape=r...]
where the time goes in v4:
time: 53.9 us; the launch traced here: 53.7 us
  Pallas kernels  53.1 us (99%)
  between operations  0.64 us (1%)
    pallas_call x1, Pallas kernels, per_device(): pl.pallas_call(functools.partial(kernel, n_dp, width, length), out_shape=...  50.8 us
    pallas_call x1, Pallas kernels, per_device(): pl.pallas_call(functools.partial(store_kernel, len(results)), out_shape=r...  2.28 us

profile of v4, /device:TPU:0, one launch (start us, length us, event | category | flops | bytes accessed | tf_op | source)
XLA Modules:
  0.0 53.7 jit_solution(12300173835102362527)
XLA Ops:
  0.6 50.8 %shard_map.121 = (bf16[512,1024]{1,0:T(8,128)(2,1)}, f32[8,64,64]{2,1,0:T(8,128)}, f32[64,1024]{1,0:T(8,128)}) custom-call(s32[8]{0:T(128)} %slot_hbm.1, bf16[512,1024]{1,0:T(8,128)(2,1)} %bitcast.7, bf16[8,64,128]{2,1,0:T(8,128)(2,1)} %k_hbm.1, bf16[8,64,128]{2,1,0:T(8,128)(2,1)} %v_hbm.1, s32[8,2,16]{2,1,0:T(2,128)} %bitcast.10, s32[8,64]{1,0:T(8,128)} %label_hbm.1, ...), custom_call_target="tpu_custom_call" | custom-call | tf_op jit(solution)/shard_map/pallas_call | solution.py:529
  51.4 2.3 %shard_map.122 = (bf16[512,1024]{1,0:T(8,128)(2,1)}, f32[8,64,64]{2,1,0:T(8,128)}, f32[64,1024]{1,0:T(8,128)}) custom-call(bf16[512,1024]{1,0:T(8,128)(2,1)} %get-tuple-element.9.refs_0_, f32[8,64,64]{2,1,0:T(8,128)} %get-tuple-element.10.refs_1_, f32[64,1024]{1,0:T(8,128)} %get-tuple-element.11.refs_2_), custom_call_target="tpu_custom_call" | custom-call | tf_op jit(solution)/shard_map/pallas_call | solution.py:550

commit v5 on v4

--- a/solution.py
+++ b/solution.py
@@ -134,7 +134,7 @@
             weight_hbm.at[:, columns], w_buf.at[place], w_sem.at[place]
         )
         w_copies.append(copy)
-    for copy in in_copies[:8] + w_copies + in_copies[8:]:
+    for copy in in_copies[:8]:
         copy.start()
 
     rows = local_heads * length
@@ -170,6 +170,8 @@
 
     for copy in in_copies[:4]:
         copy.wait()
+    for copy in w_copies + in_copies[8:]:
+        copy.start()
     index_rows = jnp.concatenate(
         [(patch_ref[j][0:1, :] - t * local_heads) * length + patch_ref[j][1:2, :] for j in every],
         axis=0,
@@ -242,34 +244,39 @@
     def project(rows, place):
         return jnp.dot(x_buf[rows, :], w_buf[place], preferred_element_type=F32).astype(BF16)
 
-    def start_a(j):
-        a_send[chunk(j), :] = project(chunk(j), 0)
-        remote(a_send, a_recv, a_sems, j, sib).start()
-
-    def start_c(j):
-        mine = project(chunk(j), 1).astype(F32)
-        remote(a_send, a_recv, a_sems, j, sib).wait()
-        c_send[chunk(j), :] = (mine + a_recv[chunk(j), :].astype(F32)).astype(BF16)
-        remote(c_send, c_recv, c_sems, j, opp).start()
-
-    patch(0)
-    w_copies[0].wait()
-    start_a(0)
-    w_copies[1].wait()
-
-    def first(j, carry):
-        patch(j + 1)
-        start_a(j + 1)
-        start_c(j)
-        return carry
-
-    done = 0
-    for low in range(ready, prompts, 2):
-        first(done, 0)
-        done += 1
-        attend(low, min(low + 2, prompts))
-    lax.fori_loop(done, prompts - 1, first, 0)
-    start_c(prompts - 1)
+    def rows_of(low, high):
+        return slice(low * length, high * length)
+
+    def start_a(low, high):
+        a_send[rows_of(low, high), :] = project(rows_of(low, high), 0)
+        for j in range(low, high):
+            remote(a_send, a_recv, a_sems, j, sib).start()
+
+    def start_c(low, high):
+        at = rows_of(low, high)
+        mine = project(at, 1).astype(F32)
+        for j in range(low, high):
+            remote(a_send, a_recv, a_sems, j, sib).wait()
+        c_send[at, :] = (mine + a_recv[at, :].astype(F32)).astype(BF16)
+        for j in range(low, high):
+            remote(c_send, c_recv, c_sems, j, opp).start()
+
+    groups = [(0, 1), (1, 2)] + [
+        (low, min(low + 2, prompts)) for low in range(2, prompts, 2)
+    ]
+    waiting = list(range(ready, prompts, 2))
+    for place, (low, high) in enumerate(groups):
+        for j in range(low, high):
+            patch(j)
+        if place < 2:
+            w_copies[place].wait()
+        start_a(low, high)
+        if place > 0:
+            start_c(*groups[place - 1])
+            if waiting:
+                attend(waiting[0], min(waiting[0] + 2, prompts))
+                waiting.pop(0)
+    start_c(*groups[-1])
     w_copies[2].wait()
     w_copies[3].wait()
     halves = d_sems.shape[1]
@@ -289,8 +296,8 @@
     lax.fori_loop(0, halves, second, 0)
     for copy in in_copies[5:]:
         copy.wait()
-    probe = probe_ref[...].astype(BF16)
-    probe_buf[...] = jnp.concatenate([probe, jnp.zeros_like(probe)], axis=0)
+    probe = probe_ref[...]
+    probe_buf[...] = jnp.concatenate([probe, jnp.zeros_like(probe)], axis=0).T.astype(BF16)
     for j in every:
         class_id = lax.broadcasted_iota(jnp.int32, (classes, length), 0)
         target = jnp.where(class_id == label_ref[j : j + 1, :], 1.0, 0.0)
@@ -321,7 +328,7 @@
         squares = jnp.sum(hidden * hidden, axis=1, keepdims=True)
         hg = (hidden * gain_ref[...]).astype(BF16)
         hg_buf[at, :] = hg
-        part = contract(hg, probe_buf[...], 1, 1)
+        part = contract(hg, probe_buf[...], 1, 0)
         l1_send[j] = pack(part, squares)
         remote(l1_send, l1_recv, l1_sems, j, sib, j).start()
 
@@ -497,7 +504,7 @@
         part,
         part,
         part,
-        pltpu.VMEM((2 * classes, block), BF16),
+        pltpu.VMEM((block, 2 * classes), BF16),
         pltpu.VMEM((prompts, length, classes), F32),
         pltpu.VMEM((tokens, classes), BF16),
         message,

time: 53.9 us -> 54 us (level)
  no operation moved by 1% of the time
where the time goes in v5:
time: 54 us; the launch traced here: 53.8 us
  Pallas kernels  53.2 us (99%)
  between operations  0.64 us (1%)
    pallas_call x1, Pallas kernels, per_device(): pl.pallas_call(functools.partial(kernel, n_dp, width, length), out_shape=...  50.9 us
    pallas_call x1, Pallas kernels, per_device(): pl.pallas_call(functools.partial(store_kernel, len(results)), out_shape=r...  2.28 us

profile of v5, /device:TPU:0, one launch (start us, length us, event | category | flops | bytes accessed | tf_op | source)
XLA Modules:
  0.0 53.8 jit_solution(5507631464801947544)
XLA Ops:
  0.6 50.9 %shard_map.121 = (bf16[512,1024]{1,0:T(8,128)(2,1)}, f32[8,64,64]{2,1,0:T(8,128)}, f32[64,1024]{1,0:T(8,128)}) custom-call(s32[8]{0:T(128)} %slot_hbm.1, bf16[512,1024]{1,0:T(8,128)(2,1)} %bitcast.7, bf16[8,64,128]{2,1,0:T(8,128)(2,1)} %k_hbm.1, bf16[8,64,128]{2,1,0:T(8,128)(2,1)} %v_hbm.1, s32[8,2,16]{2,1,0:T(2,128)} %bitcast.10, s32[8,64]{1,0:T(8,128)} %label_hbm.1, ...), custom_call_target="tpu_custom_call" | custom-call | tf_op jit(solution)/shard_map/pallas_call | solution.py:536
  51.6 2.3 %shard_map.122 = (bf16[512,1024]{1,0:T(8,128)(2,1)}, f32[8,64,64]{2,1,0:T(8,128)}, f32[64,1024]{1,0:T(8,128)}) custom-call(bf16[512,1024]{1,0:T(8,128)(2,1)} %get-tuple-element.9.refs_0_, f32[8,64,64]{2,1,0:T(8,128)} %get-tuple-element.10.refs_1_, f32[64,1024]{1,0:T(8,128)} %get-tuple-element.11.refs_2_), custom_call_target="tpu_custom_call" | custom-call | tf_op jit(solution)/shard_map/pallas_call | solution.py:557

commit v6 on v5

--- a/solution.py
+++ b/solution.py
@@ -73,6 +73,7 @@
     l1_recv,
     l2_send,
     l2_recv,
+    cross_recv,
     g_send,
     g_recv,
     ag_buf,
@@ -85,6 +86,7 @@
     d_sems,
     l1_sems,
     l2_sems,
+    cross_sem,
     rs_ssem,
     rs_rsem,
     ag_ssem,
@@ -106,6 +108,7 @@
     barrier = pltpu.get_barrier_semaphore()
     pl.semaphore_signal(barrier, inc=1, device_id=(d, sib), device_id_type=MESH)
     pl.semaphore_signal(barrier, inc=1, device_id=(d, opp), device_id_type=MESH)
+    pl.semaphore_signal(barrier, inc=1, device_id=(d, opp_sib), device_id_type=MESH)
     for off in range(1, n_dp):
         pl.semaphore_signal(
             barrier, inc=1, device_id=(lax.rem(d + off, n_dp), t), device_id_type=MESH
@@ -187,7 +190,7 @@
     for j in every:
         entry_send[j] = contract(weights[j], v_ref[j], 0, 0).astype(BF16)
 
-    pl.semaphore_wait(barrier, n_dp + 1)
+    pl.semaphore_wait(barrier, n_dp + 2)
     entry_copy = pltpu.make_async_remote_copy(
         src_ref=entry_send,
         dst_ref=entry_recv,
@@ -339,12 +342,33 @@
         l2_send[j] = pack(part_a + part_b, squares_a + squares_b)
         remote(l2_send, l2_recv, l2_sems, j, opp, j).start()
 
-    def stage5(low, high):
-        for j in range(low, high):
-            remote(l2_send, l2_recv, l2_sems, j, opp, j).wait()
+    def direct_copies(j):
+        return (
+            pltpu.make_async_remote_copy(
+                src_ref=l1_send.at[j],
+                dst_ref=l2_recv.at[j],
+                send_sem=l2_sems.at[0, j],
+                recv_sem=l2_sems.at[1, j],
+                device_id=(d, opp),
+                device_id_type=MESH,
+            ),
+            pltpu.make_async_remote_copy(
+                src_ref=l1_send.at[j],
+                dst_ref=cross_recv,
+                send_sem=cross_sem.at[0],
+                recv_sem=cross_sem.at[1],
+                device_id=(d, opp_sib),
+                device_id_type=MESH,
+            ),
+        )
+
+    def add(one, two):
+        return one[0] + two[0], one[1] + two[1]
+
+    def stage5(low, high, here, there):
         count = (high - low) * length
-        part_a, squares_a = unpack(l2_send[low:high].reshape(count, LANES))
-        part_b, squares_b = unpack(l2_recv[low:high].reshape(count, LANES))
+        part_a, squares_a = here
+        part_b, squares_b = there
         inverse = lax.rsqrt((squares_a + squares_b) / width + norm_epsilon)
         logits = (part_a + part_b)[:, :classes] * inverse
         logits_ref[low:high] = logits.reshape(high - low, length, classes)
@@ -367,11 +391,28 @@
     lax.fori_loop(1, prompts, third, 0)
     out_copies[0].start()
     last = prompts - 1
-    stage4(last)
-    stage5(0, last)
+    direct = direct_copies(last)
+    for copy in direct:
+        copy.start()
+    for j in range(last):
+        remote(l2_send, l2_recv, l2_sems, j, opp, j).wait()
     early = last * length
+    stage5(
+        0,
+        last,
+        unpack(l2_send[:last].reshape(early, LANES)),
+        unpack(l2_recv[:last].reshape(early, LANES)),
+    )
     grad = contract(err_buf[:early, :], hg_buf[:early, :], 0, 0)
-    stage5(last, prompts)
+    remote(l1_send, l1_recv, l1_sems, last, sib, last).wait()
+    for copy in direct:
+        copy.wait()
+    stage5(
+        last,
+        prompts,
+        add(unpack(l1_send[last]), unpack(l1_recv[last])),
+        add(unpack(l2_recv[last]), unpack(cross_recv[...])),
+    )
     out_copies[1].start()
     grad = grad + contract(err_buf[early:, :], hg_buf[early:, :], 0, 0)
 
@@ -401,7 +442,8 @@
             device_id_type=MESH,
         )
 
-    peers = [lax.rem(d + off, n_dp) for off in range(1, n_dp)]
+    offsets = sorted(range(1, n_dp), key=lambda off: abs(off - n_dp // 2))
+    peers = [lax.rem(d + off, n_dp) for off in offsets]
     for peer in peers:
         scatter(peer, d).start()
     g_recv[d] = g_send[d]
@@ -511,6 +553,7 @@
         message,
         message,
         message,
+        pltpu.VMEM((length, LANES), BF16),
         pieces,
         pieces,
         pieces,
@@ -523,6 +566,7 @@
         dma((2, 2)),
         dma((2, prompts)),
         dma((2, prompts)),
+        dma((2,)),
         dma((n_dp,)),
         dma((n_dp,)),
         dma((n_dp,)),

time: 54 us -> 54.7 us (1.013)
  Pallas kernels: 53.2 us -> 53.9 us
    pallas_call x1, Pallas kernels: 50.9 us -> 51.6 us  [per_device(): pl.pallas_call(functools.partial(kernel, n_dp, width, length), out_shape=...]
where the time goes in v6:
time: 54.7 us; the launch traced here: 54.5 us
  Pallas kernels  53.9 us (99%)
  between operations  0.64 us (1%)
    pallas_call x1, Pallas kernels, per_device(): pl.pallas_call(functools.partial(kernel, n_dp, width, length), out_shape=...  51.6 us
    pallas_call x1, Pallas kernels, per_device(): pl.pallas_call(functools.partial(store_kernel, len(results)), out_shape=r...  2.28 us

profile of v6, /device:TPU:0, one launch (start us, length us, event | category | flops | bytes accessed | tf_op | source)
XLA Modules:
  0.0 54.5 jit_solution(10985515387234253687)
XLA Ops:
  0.6 51.6 %shard_map.121 = (bf16[512,1024]{1,0:T(8,128)(2,1)}, f32[8,64,64]{2,1,0:T(8,128)}, f32[64,1024]{1,0:T(8,128)}) custom-call(s32[8]{0:T(128)} %slot_hbm.1, bf16[512,1024]{1,0:T(8,128)(2,1)} %bitcast.7, bf16[8,64,128]{2,1,0:T(8,128)(2,1)} %k_hbm.1, bf16[8,64,128]{2,1,0:T(8,128)(2,1)} %v_hbm.1, s32[8,2,16]{2,1,0:T(2,128)} %bitcast.10, s32[8,64]{1,0:T(8,128)} %label_hbm.1, ...), custom_call_target="tpu_custom_call" | custom-call | tf_op jit(solution)/shard_map/pallas_call | solution.py:580
  52.3 2.3 %shard_map.122 = (bf16[512,1024]{1,0:T(8,128)(2,1)}, f32[8,64,64]{2,1,0:T(8,128)}, f32[64,1024]{1,0:T(8,128)}) custom-call(bf16[512,1024]{1,0:T(8,128)(2,1)} %get-tuple-element.9.refs_0_, f32[8,64,64]{2,1,0:T(8,128)} %get-tuple-element.10.refs_1_, f32[64,1024]{1,0:T(8,128)} %get-tuple-element.11.refs_2_), custom_call_target="tpu_custom_call" | custom-call | tf_op jit(solution)/shard_map/pallas_call | solution.py:601
